TPU v7x, 256 devices: a whole 4x4x8 slice. The times are simulated.
256 devices in a mesh: fsdp: 16 (over x, y), tp: 16 (over z, core).
Axes of the slice: x: 4, y: 4, z: 8, core: 2. Of those that a mesh axis runs over, the one named last changes fastest.
Arguments:
- momentum: bfloat16 [8192, 26624], P('fsdp', 'tp'), may hold values from -6 to 6
- gradient: bfloat16 [8192, 26624], P('fsdp', 'tp'), may hold values from -3 to 3
- basis: bfloat16 [26624, 256], P('tp'), may hold values from -0.010663815 to 0.010663815
Outputs:
- momentum_next: bfloat16 [8192, 26624], P('fsdp', 'tp')
- basis_next: bfloat16 [26624, 256], P('tp')
- update: bfloat16 [8192, 26624], P('fsdp', 'tp')
All inputs are finite; a program needn't handle non-finite values.
Results may differ from a plain program's by a relative error of at most 0.009.
Values may be sent and summed in bfloat16 or wider, within the bound.
No kernel may reach another device: no remote copies, remote signals or barrier semaphores. Data moves between devices by JAX's collectives and lax.ppermute only.
A program may use at most 64 MiB of HBM per device.

v0:
```python
import functools

import jax
import jax.numpy as jnp
from jax import lax
from jax.experimental import pallas as pl
from jax.experimental.pallas import tpu as pltpu
from jax.sharding import PartitionSpec as P

M_ROWS = 8192
N_COLS = 26624
RANK = 256
SCALE = (M_ROWS * N_COLS / RANK) ** 0.5
F32, BF16 = jnp.float32, jnp.bfloat16
PANEL = 64
VMEM = pl.BlockSpec(memory_space=pltpu.VMEM)
HBM = pl.BlockSpec(memory_space=pltpu.HBM)
TERMS = 2
ROWS_BY_ROWS = (((0,), (0,)), ((), ()))
COLS_BY_COLS = (((1,), (1,)), ((), ()))
ROWS_BY_COLS = (((1,), (0,)), ((), ()))


def iota(shape, dim):
    return lax.broadcasted_iota(jnp.int32, shape, dim)


def shape(dims, dtype=F32):
    return jax.ShapeDtypeStruct(dims, dtype)


def held(dims, dtype=F32):
    return pltpu.VMEM(dims, dtype)


def call(body, out, name, *args, scratch=(), flops=0, out_specs=None):
    many = isinstance(out, (list, tuple))
    return pl.pallas_call(
        body,
        out_shape=out,
        in_specs=[VMEM] * len(args),
        out_specs=out_specs or ([VMEM] * len(out) if many else VMEM),
        scratch_shapes=list(scratch),
        compiler_params=pltpu.CompilerParams(vmem_limit_bytes=24 << 20),
        cost_estimate=pl.CostEstimate(flops=flops, bytes_accessed=1 << 20, transcendentals=0),
        name=name,
    )(*(pltpu.with_memory_space_constraint(a, pltpu.VMEM) for a in args))


def split(value):
    high = value.astype(BF16)
    rest = value - high.astype(F32)
    mid = rest.astype(BF16)
    return high, mid, (rest - mid.astype(F32)).astype(BF16)


def left_terms(value, axis):
    high, mid, low = split(value)
    return jnp.concatenate([high, high, mid, mid, high, low], axis=axis)


def right_terms(value):
    high, mid, low = split(value)
    return jnp.concatenate([high, mid, high, mid, low, high], axis=0)


def pieces_of(cols):
    cuts = [0, -(-cols // 384) * 128, -(-2 * cols // 384) * 128, cols]
    return list(zip(cuts[:-1], cuts[1:]))


def blend_body(momentum_ref, gradient_ref, basis_ref, blended_ref, left_ref, m_ref, g_ref, b_ref, sems):
    pieces = []
    for i, (lo, hi) in enumerate(pieces_of(blended_ref.shape[1])):
        lanes, rows = (slice(None), pl.ds(lo, hi - lo)), (pl.ds(lo, hi - lo), slice(None))
        copies = [
            pltpu.make_async_copy(src.at[at], dst.at[at], sems.at[3 * i + k])
            for k, (src, dst, at) in enumerate(
                ((momentum_ref, m_ref, lanes), (gradient_ref, g_ref, lanes), (basis_ref, b_ref, rows))
            )
        ]
        for copy in copies:
            copy.start()
        pieces.append((lo, hi, copies))
    left = None
    for lo, hi, copies in pieces:
        for copy in copies:
            copy.wait()
        blended = (m_ref[:, lo:hi].astype(F32) + g_ref[:, lo:hi].astype(F32)).astype(BF16)
        blended_ref[:, lo:hi] = blended
        part = jnp.dot(blended, b_ref[lo:hi, :], preferred_element_type=F32)
        left = part if left is None else left + part
    left_ref[...] = left.astype(BF16)


def blend(momentum, gradient, basis):
    rows, cols = momentum.shape
    rank = basis.shape[1]
    return pl.pallas_call(
        blend_body,
        out_shape=[held((rows, cols), BF16), held((rows, rank), BF16)],
        in_specs=[HBM] * 3,
        out_specs=[VMEM] * 2,
        scratch_shapes=[
            pltpu.VMEM((rows, cols), BF16),
            pltpu.VMEM((rows, cols), BF16),
            pltpu.VMEM((cols, rank), BF16),
            pltpu.SemaphoreType.DMA((9,)),
        ],
        compiler_params=pltpu.CompilerParams(vmem_limit_bytes=24 << 20),
        name="blend",
    )(*(pltpu.with_memory_space_constraint(a, pltpu.HBM) for a in (momentum, gradient, basis)))


def left_sum_body(parts_ref, out_ref):
    total = parts_ref[0].astype(F32)
    for i in range(1, parts_ref.shape[0]):
        total = total + parts_ref[i].astype(F32)
    low = total.astype(BF16)
    for i in range(out_ref.shape[0]):
        out_ref[i] = low


def project_body(blended_ref, left_ref, out_ref, work_ref):
    parts = out_ref.shape[0]
    rank = left_ref.shape[1]
    some = rank // parts
    block = blended_ref.shape[1] // parts
    left = left_ref[...]
    gram = split(lax.dot_general(left, left, ROWS_BY_ROWS, preferred_element_type=F32))[:TERMS]
    work_ref[...] = lax.dot_general(blended_ref[...], left, ROWS_BY_ROWS, preferred_element_type=F32)
    for f in range(parts):
        for i, term in enumerate(gram):
            out_ref[f, i * some : (i + 1) * some, :] = term[f * some : (f + 1) * some]
        out_ref[f, TERMS * some :, :] = work_ref[f * block : (f + 1) * block, :].astype(BF16)


def project_sum_body(parts_ref, out_ref, *, some):
    total = parts_ref[0].astype(F32)
    for i in range(1, parts_ref.shape[0]):
        total = total + parts_ref[i].astype(F32)
    high, low, _ = split(total[some : 2 * some] + total[:some])
    merged = jnp.concatenate([high, low, total[TERMS * some :].astype(BF16)], axis=0)
    for i in range(out_ref.shape[0]):
        out_ref[i] = merged


def diag_inverse(block):
    b = block.shape[0]
    n, width = b // 8, 2 * b
    eye = iota((b, b), 0) == iota((b, b), 1)
    aug = jnp.concatenate([block, jnp.where(eye, 1.0, 0.0)], axis=1)
    sub = iota((8, width), 0)
    rows = [aug[8 * i : 8 * i + 8] for i in range(n)]

    def spread(value, m):
        return jnp.broadcast_to(value[m : m + 1], (8, width))

    for g in range(n):
        cols = [
            [jnp.broadcast_to(rows[v][:, 8 * g + k : 8 * g + k + 1], (8, width)) for v in range(g, n)] for k in range(8)
        ]
        own, pivots, updates = rows[g], jnp.zeros((8, width), F32), []
        for m in range(0, 8, 2):
            first, second = cols[m], cols[m + 1]
            a, c, d = spread(first[0], m), spread(first[0], m + 1), spread(second[0], m + 1)
            det = a * d - c * c
            one_a, one_det = 1.0 / a, 1.0 / det
            pivots = jnp.where(sub == m, a, jnp.where(sub == m + 1, det * one_a, pivots))
            ia, ic, id_ = d * one_det, c * one_det, a * one_det
            below = sub > m + 1
            f0, f1 = jnp.where(below, first[0], 0.0), jnp.where(below, second[0], 0.0)

            def solved(value):
                x0, x1 = spread(value, m), spread(value, m + 1)
                return ia * x0 - ic * x1, id_ * x1 - ic * x0

            s0, s1 = solved(own)
            own = own - (f0 * s0 + f1 * s1) - jnp.where(sub == m + 1, c * one_a * spread(own, m), 0.0)
            updates += [(first[1:], s0), (second[1:], s1)]
            for k in range(m + 2, 8):
                t0, t1 = solved(cols[k][0])
                cols[k][0] = cols[k][0] - (f0 * t0 + f1 * t1)
                for v in range(1, n - g):
                    cols[k][v] = cols[k][v] - (first[v] * t0 + second[v] * t1)
        rows[g] = own * lax.rsqrt(pivots)
        for v in range(1, n - g):
            rows[g + v] = rows[g + v] - sum(col[v - 1] * s for col, s in updates)
    return jnp.concatenate(rows, axis=0)[:, b:]


def inverse_factor(gram, inv_ref):
    rank = gram.shape[0]
    row, col = iota((rank, rank), 0), iota((rank, rank), 1)
    inv_ref[...] = gram + jnp.where(row == col, 0.001, 0.0)
    lanes = iota((1, rank), 1)
    for p in range(0, rank, PANEL):
        q = p + PANEL
        inverse = diag_inverse(inv_ref[p:q, p:q])
        full = jnp.dot(left_terms(inverse, 1), right_terms(inv_ref[p:q, :]), preferred_element_type=F32)
        pieces = [full[:, :p]] if p else []
        pieces.append(inverse)
        if q < rank:
            pieces.append(full[:, q:])
        panel = jnp.concatenate(pieces, axis=1)
        inv_ref[p:q, :] = panel
        if q < rank:
            change = lax.dot_general(
                left_terms(panel[:, q:], 0), right_terms(panel), ROWS_BY_ROWS, preferred_element_type=F32
            )
            inv_ref[q:, :] = jnp.where((lanes >= p) & (lanes < q), 0.0, inv_ref[q:, :]) - change
    inv_ref[...] = jnp.where(row >= col, inv_ref[...], 0.0)


def by_inverse(low, inverse):
    n = inverse.shape[0]
    terms = jnp.concatenate(split(inverse)[:TERMS], axis=0)
    parts = lax.dot_general(low, terms, COLS_BY_COLS, preferred_element_type=F32)
    return parts[:, :n] + parts[:, n:]


def product(a, b, dims, terms):
    if terms == 1:
        return lax.dot_general(a.astype(BF16), b.astype(BF16), dims, preferred_element_type=F32)
    (a_high, a_low, _), (b_high, b_low, _) = split(a), split(b)
    a = jnp.concatenate([a_high, a_high, a_low], axis=dims[0][0][0])
    b = jnp.concatenate([b_high, b_low, b_high], axis=dims[0][1][0])
    return lax.dot_general(a, b, dims, preferred_element_type=F32)


def refined_factor(gram, inv_ref):
    rank = gram.shape[0]
    row, col = iota((rank, rank), 0), iota((rank, rank), 1)
    eye = row == col
    gram = gram + jnp.where(eye, 0.001, 0.0)
    diag = jnp.where(eye, gram, 0.0)
    scale = lax.rsqrt(jnp.sum(diag, axis=0, keepdims=True))
    gram = gram * lax.rsqrt(jnp.sum(diag, axis=1, keepdims=True)) * scale
    inverse = jnp.where(eye, 1.0, jnp.where(row > col, -gram, 0.0))
    for terms in (1, 2, 2):
        error = product(product(inverse, gram, ROWS_BY_COLS, terms), inverse, COLS_BY_COLS, terms)
        error = error - jnp.where(eye, 1.0, 0.0)
        lower = jnp.where(row > col, error, jnp.where(eye, 0.5 * error, 0.0))
        inverse = inverse - product(lower, inverse, ROWS_BY_COLS, terms)
    inv_ref[...] = inverse * scale
    return jnp.sum(error * error)


def factor_body(parts_ref, inv_ref, proj_ref, colsq_ref):
    rank = inv_ref.shape[0]
    some = rank // parts_ref.shape[0]
    gram = parts_ref[:, :some, :].astype(F32) + parts_ref[:, some : 2 * some, :].astype(F32)
    gram = gram.reshape(rank, rank)
    proj_ref[...] = parts_ref[:, TERMS * some :, :].astype(F32).reshape(proj_ref.shape).astype(BF16)

    taken = refined_factor(gram, inv_ref)

    @pl.when(jnp.logical_not(taken < 1e-4))
    def _():
        inverse_factor(gram, inv_ref)

    right = by_inverse(proj_ref[...], inv_ref[...])
    colsq = jnp.broadcast_to(jnp.sum(right * right, axis=0, keepdims=True), colsq_ref.shape[1:])
    for i in range(colsq_ref.shape[0]):
        colsq_ref[i] = colsq


def feedback_body(blended_ref, left_ref, proj_ref, inv_ref, momentum_ref, ortho_ref):
    ortho_ref[...] = by_inverse(left_ref[...], inv_ref[...]).astype(BF16)
    right = by_inverse(proj_ref[...], inv_ref[...])
    feedback = lax.dot_general(ortho_ref[...], right.astype(BF16), COLS_BY_COLS, preferred_element_type=F32)
    momentum_ref[...] = (blended_ref[...].astype(F32) - 0.1 * feedback).astype(BF16)


def update_body(ortho_ref, proj_ref, inv_ref, colsq_ref, update_ref, basis_ref, product_ref, next_ref, sems):
    colsq = colsq_ref[0, 0:1, :]
    for i in range(1, colsq_ref.shape[0]):
        colsq = colsq + colsq_ref[i, 0:1, :]
    scale = lax.rsqrt(colsq + 1e-06)
    inverse, ortho, copies = inv_ref[...], ortho_ref[...], []
    for lo, hi in pieces_of(product_ref.shape[1]):
        rows, lanes = (pl.ds(lo, hi - lo), slice(None)), (slice(None), pl.ds(lo, hi - lo))
        basis = (by_inverse(proj_ref[lo:hi, :], inverse) * scale).astype(BF16)
        next_ref[lo:hi, :] = basis
        copies.append(pltpu.make_async_copy(next_ref.at[rows], basis_ref.at[rows], sems.at[len(copies)]))
        copies[-1].start()
        product = lax.dot_general(ortho, basis, COLS_BY_COLS, preferred_element_type=F32)
        product_ref[:, lo:hi] = (SCALE * product).astype(BF16)
        copies.append(pltpu.make_async_copy(product_ref.at[lanes], update_ref.at[lanes], sems.at[len(copies)]))
        copies[-1].start()
    for copy in copies:
        copy.wait()


def on_device(momentum, gradient, basis, n_fsdp, n_tp):
    rank = basis.shape[1]
    rows, cols = momentum.shape
    some, block = rank // n_fsdp, cols // n_fsdp

    def exchange(parts, axis):
        return lax.all_to_all(parts, axis, 0, 0, tiled=True)

    blended, left = blend(momentum, gradient, basis)
    parts = exchange(left.reshape(n_tp, rows // n_tp, rank), "tp")
    spread = call(left_sum_body, held(parts.shape, BF16), "left_sum", parts)
    left = exchange(spread, "tp").reshape(rows, rank)

    sent = held((n_fsdp, TERMS * some + block, rank), BF16)
    parts = call(project_body, sent, "project", blended, left, scratch=[pltpu.VMEM((cols, rank), F32)])
    merged = call(
        functools.partial(project_sum_body, some=some), held(parts.shape, BF16), "project_sum", exchange(parts, "fsdp")
    )
    inverse, proj, colsq = call(
        factor_body,
        [held((rank, rank)), held((cols, rank), BF16), held((n_tp, 8, rank))],
        "factor",
        exchange(merged, "fsdp"),
    )
    colsq = exchange(colsq, "tp")
    momentum_next, ortho = call(
        feedback_body,
        [shape((rows, cols), BF16), held((rows, rank), BF16)],
        "feedback",
        blended,
        left,
        proj,
        inverse,
    )
    update_next, basis_next = call(
        update_body,
        [pltpu.HBM((rows, cols), BF16), pltpu.HBM((cols, rank), BF16)],
        "update",
        ortho,
        proj,
        inverse,
        colsq,
        scratch=[pltpu.VMEM((rows, cols), BF16), pltpu.VMEM((cols, rank), BF16), pltpu.SemaphoreType.DMA((6,))],
        out_specs=[HBM, HBM],
    )
    return momentum_next, basis_next, update_next


def solution(mesh):
    body = functools.partial(on_device, n_fsdp=mesh.shape["fsdp"], n_tp=mesh.shape["tp"])
    return jax.shard_map(
        body,
        mesh=mesh,
        in_specs=(P("fsdp", "tp"), P("fsdp", "tp"), P("tp", None)),
        out_specs=(P("fsdp", "tp"), P("tp", None), P("fsdp", "tp")),
        check_vma=False,
    )
```

profile of v0, /device:TPU:1, one launch (start us, length us, event | category | flops | bytes accessed | tf_op | source)
XLA Modules:
  0.0 105.2 jit_solution(5698362669642548764)
XLA Ops:
  0.6 2.9 %blend.1 = (bf16[512,1664]{1,0:T(8,128)(2,1)S(1)}, bf16[512,256]{1,0:T(8,128)(2,1)S(1)}) custom-call(bf16[512,1664]{1,0:T(8,128)(2,1)} %momentum_ref.1, bf16[512,1664]{1,0:T(8,128)(2,1)} %gradient_ref.1, bf16[1664,256]{1,0:T(8,128)(2,1)} %basis_ref.1), custom_call_target="tpu_custom_call" | custom-call | tf_op jit(solution)/shard_map/blend/pallas_call | solution.py:99
  3.5 21.5 %all_to_all.25.parts_ref = bf16[16,32,256]{2,1,0:T(8,128)(2,1)S(1)} all-to-all(bf16[16,32,256]{2,1,0:T(8,128)(2,1)S(1)} %bitcast.4), channel_id=1, replica_groups=mesh['fsdp'=16,'tp'=16] {'tp'}, dimensions={0} | all-to-all | bytes 524288 | tf_op jit(solution)/shard_map/all_to_all | solution.py:301
  25.1 14.4 %all_to_all.26 = bf16[16,32,256]{2,1,0:T(8,128)(2,1)S(1)} all-to-all(bf16[16,32,256]{2,1,0:T(8,128)(2,1)S(1)} %left_sum.1), channel_id=1, replica_groups=mesh['fsdp'=16,'tp'=16] {'tp'}, dimensions={0} | all-to-all | bytes 524288 | tf_op jit(solution)/shard_map/all_to_all | solution.py:301
  39.5 0.7 project.1
  40.2 24.4 %all_to_all.27.parts_ref = bf16[16,136,256]{2,1,0:T(8,128)(2,1)S(1)} all-to-all(bf16[16,136,256]{2,1,0:T(8,128)(2,1)S(1)} %project.1), channel_id=1, replica_groups=mesh['fsdp'=16,'tp'=16] {'fsdp'}, dimensions={0} | all-to-all | bytes 2228224 | tf_op jit(solution)/shard_map/all_to_all | solution.py:301
  64.6 0.2 project_sum.1
  64.8 19.5 %all_to_all.28.parts_ref = bf16[16,136,256]{2,1,0:T(8,128)(2,1)S(1)} all-to-all(bf16[16,136,256]{2,1,0:T(8,128)(2,1)S(1)} %project_sum.1), channel_id=1, replica_groups=mesh['fsdp'=16,'tp'=16] {'fsdp'}, dimensions={0} | all-to-all | bytes 2228224 | tf_op jit(solution)/shard_map/all_to_all | solution.py:301
  84.2 3.4 %factor.1 = (f32[256,256]{1,0:T(8,128)S(1)}, bf16[1664,256]{1,0:T(8,128)(2,1)S(1)}, f32[16,8,256]{2,1,0:T(8,128)}) custom-call(bf16[16,136,256]{2,1,0:T(8,128)(2,1)S(1)} %all_to_all.28.parts_ref), custom_call_target="tpu_custom_call" | custom-call | bytes 1048576 | tf_op jit(solution)/shard_map/factor/pallas_call | solution.py:38
  87.7 5.8 %all-to-all-start.4 = ((f32[16,8,256]{2,1,0:T(8,128)}), f32[16,8,256]{2,1,0:T(8,128)S(1)}, u32[]{:S(2)}, u32[]{:S(2)}) async-start(f32[16,8,256]{2,1,0:T(8,128)} %get-tuple-element.18), calls=%async_computation.4 | async-start | bytes 262144 | tf_op jit(solution)/shard_map/all_to_all | solution.py:301
  93.4 2.8 %feedback.1 = (bf16[512,1664]{1,0:T(8,128)(2,1)}, bf16[512,256]{1,0:T(8,128)(2,1)S(1)}) custom-call(bf16[512,1664]{1,0:T(8,128)(2,1)S(1)} %get-tuple-element.12.blended_ref, bf16[512,256]{1,0:T(8,128)(2,1)S(1)} %bitcast.3, bf16[1664,256]{1,0:T(8,128)(2,1)S(1)} %get-tuple-element.14.proj_ref, f32[256,256]{1,0:T(8,128)S(1)} %get-tuple-element.15.inv_ref), custom_call_target="tpu_custom_call" | custom-call | bytes 1048576 | tf_op jit(solution)/shard_map/feedback/pallas_call | solution.py:38
  96.2 6.4 %all-to-all-done.4.colsq_ref = f32[16,8,256]{2,1,0:T(8,128)S(1)} async-done(((f32[16,8,256]{2,1,0:T(8,128)}), f32[16,8,256]{2,1,0:T(8,128)S(1)}, u32[]{:S(2)}, u32[]{:S(2)}) %all-to-all-start.4) | async-done | bytes 131104 | tf_op jit(solution)/shard_map/all_to_all | solution.py:301
  102.7 2.4 %update.1 = (bf16[512,1664]{1,0:T(8,128)(2,1)}, bf16[1664,256]{1,0:T(8,128)(2,1)}) custom-call(bf16[512,256]{1,0:T(8,128)(2,1)S(1)} %get-tuple-element.17.ortho_ref, bf16[1664,256]{1,0:T(8,128)(2,1)S(1)} %get-tuple-element.14.proj_ref, f32[256,256]{1,0:T(8,128)S(1)} %get-tuple-element.15.inv_ref, f32[16,8,256]{2,1,0:T(8,128)S(1)} %all-to-all-done.4.colsq_ref), custom_call_target="tpu_custom_call" | custom-call | bytes 1048576 | tf_op jit(solution)/shard_map/update/pallas_call | solution.py:38
  (1 shorter events, 0.0 us)
Async XLA Ops:
  87.7 15.0 %all-to-all-start.4 = ((f32[16,8,256]{2,1,0:T(8,128)}), f32[16,8,256]{2,1,0:T(8,128)S(1)}, u32[]{:S(2)}, u32[]{:S(2)}) async-start(f32[16,8,256]{2,1,0:T(8,128)} %get-tuple-element.18), calls=%async_computation.4 | async-start | bytes 262144 | tf_op jit(solution)/shard_map/all_to_all | solution.py:301
where the time goes:
time: 106 us; the launch traced here: 105 us
  blocking collectives  79.8 us (75%)
  Pallas kernels  12.4 us (12%)
  waiting for transfers between devices  6.43 us (6%)
  starting transfers between devices  5.75 us (5%)
    all_to_all x4, blocking collectives, exchange(): return lax.all_to_all(parts, axis, 0, 0, tiled=True)  79.8 us
    pallas_call x6, Pallas kernels, call(): pl.pallas_call(body, out_shape=out, in_specs=[VMEM] * len(args), out_spec...  9.5 us
    all_to_all x1, waiting for transfers between devices, exchange(): return lax.all_to_all(parts, axis, 0, 0, tiled=True)  6.43 us
    all_to_all x1, starting transfers between devices, exchange(): return lax.all_to_all(parts, axis, 0, 0, tiled=True)  5.75 us
    pallas_call x1, Pallas kernels, blend(): pl.pallas_call(blend_body, out_shape=[held((rows, cols), BF16), held((row...  2.91 us
  transfers between devices with their start and end apart: 1, of which 1 were waited for; matrix products, arithmetic and copies ran while one was open for 0% of the time, Pallas kernels for 3%

commit v1 on v0

--- a/solution.py
+++ b/solution.py
@@ -16,6 +16,10 @@
 VMEM = pl.BlockSpec(memory_space=pltpu.VMEM)
 HBM = pl.BlockSpec(memory_space=pltpu.HBM)
 TERMS = 2
+ORDERS = {
+    "fsdp": [2, 11, 3, 10, 0, 4, 15, 7, 12, 1, 13, 5, 14, 9, 6, 8],
+    "tp": [11, 15, 9, 1, 12, 2, 14, 10, 0, 4, 7, 6, 13, 5, 3, 8],
+}
 ROWS_BY_ROWS = (((0,), (0,)), ((), ()))
 COLS_BY_COLS = (((1,), (1,)), ((), ()))
 ROWS_BY_COLS = (((1,), (0,)), ((), ()))
@@ -64,8 +68,8 @@
     return jnp.concatenate([high, mid, high, mid, low, high], axis=0)
 
 
-def pieces_of(cols):
-    cuts = [0, -(-cols // 384) * 128, -(-2 * cols // 384) * 128, cols]
+def pieces_of(cols, eighths=(0, 3, 6, 8)):
+    cuts = [-(-cols * e // 1024) * 128 for e in eighths[:-1]] + [cols]
     return list(zip(cuts[:-1], cuts[1:]))
 
 
@@ -213,10 +217,10 @@
 
 
 def by_inverse(low, inverse):
-    n = inverse.shape[0]
-    terms = jnp.concatenate(split(inverse)[:TERMS], axis=0)
-    parts = lax.dot_general(low, terms, COLS_BY_COLS, preferred_element_type=F32)
-    return parts[:, :n] + parts[:, n:]
+    terms = split(inverse)[:TERMS]
+    return lax.dot_general(
+        jnp.concatenate([low] * TERMS, axis=1), jnp.concatenate(terms, axis=1), COLS_BY_COLS, preferred_element_type=F32
+    )
 
 
 def product(a, b, dims, terms):
@@ -253,16 +257,19 @@
     gram = gram.reshape(rank, rank)
     proj_ref[...] = parts_ref[:, TERMS * some :, :].astype(F32).reshape(proj_ref.shape).astype(BF16)
 
+    def spread_colsq():
+        right = by_inverse(proj_ref[...], inv_ref[...])
+        colsq = jnp.broadcast_to(jnp.sum(right * right, axis=0, keepdims=True), colsq_ref.shape[1:])
+        for i in range(colsq_ref.shape[0]):
+            colsq_ref[i] = colsq
+
     taken = refined_factor(gram, inv_ref)
+    spread_colsq()
 
     @pl.when(jnp.logical_not(taken < 1e-4))
     def _():
         inverse_factor(gram, inv_ref)
-
-    right = by_inverse(proj_ref[...], inv_ref[...])
-    colsq = jnp.broadcast_to(jnp.sum(right * right, axis=0, keepdims=True), colsq_ref.shape[1:])
-    for i in range(colsq_ref.shape[0]):
-        colsq_ref[i] = colsq
+        spread_colsq()
 
 
 def feedback_body(blended_ref, left_ref, proj_ref, inv_ref, momentum_ref, ortho_ref):
@@ -278,7 +285,7 @@
         colsq = colsq + colsq_ref[i, 0:1, :]
     scale = lax.rsqrt(colsq + 1e-06)
     inverse, ortho, copies = inv_ref[...], ortho_ref[...], []
-    for lo, hi in pieces_of(product_ref.shape[1]):
+    for lo, hi in pieces_of(product_ref.shape[1], (0, 1, 3, 5, 8)):
         rows, lanes = (pl.ds(lo, hi - lo), slice(None)), (slice(None), pl.ds(lo, hi - lo))
         basis = (by_inverse(proj_ref[lo:hi, :], inverse) * scale).astype(BF16)
         next_ref[lo:hi, :] = basis
@@ -298,7 +305,7 @@
     some, block = rank // n_fsdp, cols // n_fsdp
 
     def exchange(parts, axis):
-        return lax.all_to_all(parts, axis, 0, 0, tiled=True)
+        return lax.all_to_all(parts, axis, 0, 0, tiled=True, axis_index_groups=[ORDERS[axis]])
 
     blended, left = blend(momentum, gradient, basis)
     parts = exchange(left.reshape(n_tp, rows // n_tp, rank), "tp")
@@ -334,7 +341,7 @@
         proj,
         inverse,
         colsq,
-        scratch=[pltpu.VMEM((rows, cols), BF16), pltpu.VMEM((cols, rank), BF16), pltpu.SemaphoreType.DMA((6,))],
+        scratch=[pltpu.VMEM((rows, cols), BF16), pltpu.VMEM((cols, rank), BF16), pltpu.SemaphoreType.DMA((8,))],
         out_specs=[HBM, HBM],
     )
     return momentum_next, basis_next, update_next

time: 106 us -> 97.3 us (0.918)
  blocking collectives: 79.8 us -> 69.1 us
  starting transfers between devices: 5.75 us -> 13.1 us
  waiting for transfers between devices: 6.43 us -> 1.69 us
    all_to_all x4, blocking collectives: 79.8 us -> 69.1 us  [exchange(): lax.all_to_all(parts, axis, 0, 0, tiled=True, axis_index_groups=[ORDERS[a...]
    all_to_all x1, starting transfers between devices: 5.75 us -> 13.1 us  [exchange(): lax.all_to_all(parts, axis, 0, 0, tiled=True, axis_index_groups=[ORDERS[a...]
    all_to_all x1, waiting for transfers between devices: 6.43 us -> 1.69 us  [exchange(): lax.all_to_all(parts, axis, 0, 0, tiled=True, axis_index_groups=[ORDERS[a...]
where the time goes in v1:
time: 97.3 us; the launch traced here: 96.9 us
  blocking collectives  69.1 us (71%)
  starting transfers between devices  13.1 us (13%)
  Pallas kernels  12.2 us (13%)
  waiting for transfers between devices  1.69 us (2%)
    all_to_all x4, blocking collectives, exchange(): lax.all_to_all(parts, axis, 0, 0, tiled=True, axis_index_groups=[ORDERS[a...  69.1 us
    all_to_all x1, starting transfers between devices, exchange(): lax.all_to_all(parts, axis, 0, 0, tiled=True, axis_index_groups=[ORDERS[a...  13.1 us
    pallas_call x6, Pallas kernels, call(): pl.pallas_call(body, out_shape=out, in_specs=[VMEM] * len(args), out_spec...  9.37 us
    pallas_call x1, Pallas kernels, blend(): pl.pallas_call(blend_body, out_shape=[held((rows, cols), BF16), held((row...  2.84 us
  transfers between devices with their start and end apart: 1, of which 1 were waited for; matrix products, arithmetic and copies ran while one was open for 0% of the time, Pallas kernels for 3%

profile of v1, /device:TPU:1, one launch (start us, length us, event | category | flops | bytes accessed | tf_op | source)
XLA Modules:
  0.0 96.9 jit_solution(6343702570564803050)
XLA Ops:
  0.6 2.8 %blend.1 = (bf16[512,1664]{1,0:T(8,128)(2,1)S(1)}, bf16[512,256]{1,0:T(8,128)(2,1)S(1)}) custom-call(bf16[512,1664]{1,0:T(8,128)(2,1)} %momentum_ref.1, bf16[512,1664]{1,0:T(8,128)(2,1)} %gradient_ref.1, bf16[1664,256]{1,0:T(8,128)(2,1)} %basis_ref.1), custom_call_target="tpu_custom_call" | custom-call | tf_op jit(solution)/shard_map/blend/pallas_call | solution.py:103
  3.5 16.9 %all_to_all.25.parts_ref = bf16[16,32,256]{2,1,0:T(8,128)(2,1)S(1)} all-to-all(bf16[16,32,256]{2,1,0:T(8,128)(2,1)S(1)} %bitcast.4), channel_id=1, replica_groups={{11,15,9,1,12,2,14,10,0,4,7,6,13,5,3,8},{27,31,25,17,28,18,30,26,16,20,..., dimensions={0} | all-to-all | bytes 524288 | tf_op jit(solution)/shard_map/all_to_all | solution.py:308
  20.4 14.0 %all_to_all.26 = bf16[16,32,256]{2,1,0:T(8,128)(2,1)S(1)} all-to-all(bf16[16,32,256]{2,1,0:T(8,128)(2,1)S(1)} %left_sum.1), channel_id=1, replica_groups={{11,15,9,1,12,2,14,10,0,4,7,6,13,5,3,8},{27,31,25,17,28,18,30,26,16,20,..., dimensions={0} | all-to-all | bytes 524288 | tf_op jit(solution)/shard_map/all_to_all | solution.py:308
  34.4 0.7 project.1
  35.1 21.0 %all_to_all.27.parts_ref = bf16[16,136,256]{2,1,0:T(8,128)(2,1)S(1)} all-to-all(bf16[16,136,256]{2,1,0:T(8,128)(2,1)S(1)} %project.1), channel_id=1, replica_groups={{32,176,48,160,0,64,240,112,192,16,208,80,224,144,96,128},{33,177,49,16..., dimensions={0} | all-to-all | bytes 2228224 | tf_op jit(solution)/shard_map/all_to_all | solution.py:308
  56.1 0.2 project_sum.1
  56.3 17.3 %all_to_all.28.parts_ref = bf16[16,136,256]{2,1,0:T(8,128)(2,1)S(1)} all-to-all(bf16[16,136,256]{2,1,0:T(8,128)(2,1)S(1)} %project_sum.1), channel_id=1, replica_groups={{32,176,48,160,0,64,240,112,192,16,208,80,224,144,96,128},{33,177,49,16..., dimensions={0} | all-to-all | bytes 2228224 | tf_op jit(solution)/shard_map/all_to_all | solution.py:308
  73.5 3.4 %factor.1 = (f32[256,256]{1,0:T(8,128)S(1)}, bf16[1664,256]{1,0:T(8,128)(2,1)S(1)}, f32[16,8,256]{2,1,0:T(8,128)}) custom-call(bf16[16,136,256]{2,1,0:T(8,128)(2,1)S(1)} %all_to_all.28.parts_ref), custom_call_target="tpu_custom_call" | custom-call | bytes 1048576 | tf_op jit(solution)/shard_map/factor/pallas_call | solution.py:42
  76.9 13.1 %all-to-all-start.4 = ((f32[16,8,256]{2,1,0:T(8,128)}), f32[16,8,256]{2,1,0:T(8,128)S(1)}, u32[]{:S(2)}, u32[]{:S(2)}) async-start(f32[16,8,256]{2,1,0:T(8,128)} %get-tuple-element.18), calls=%async_computation.4 | async-start | bytes 262144 | tf_op jit(solution)/shard_map/all_to_all | solution.py:308
  90.0 2.8 %feedback.1 = (bf16[512,1664]{1,0:T(8,128)(2,1)}, bf16[512,256]{1,0:T(8,128)(2,1)S(1)}) custom-call(bf16[512,1664]{1,0:T(8,128)(2,1)S(1)} %get-tuple-element.12.blended_ref, bf16[512,256]{1,0:T(8,128)(2,1)S(1)} %bitcast.3, bf16[1664,256]{1,0:T(8,128)(2,1)S(1)} %get-tuple-element.14.proj_ref, f32[256,256]{1,0:T(8,128)S(1)} %get-tuple-element.15.inv_ref), custom_call_target="tpu_custom_call" | custom-call | bytes 1048576 | tf_op jit(solution)/shard_map/feedback/pallas_call | solution.py:42
  92.8 1.7 %all-to-all-done.4.colsq_ref = f32[16,8,256]{2,1,0:T(8,128)S(1)} async-done(((f32[16,8,256]{2,1,0:T(8,128)}), f32[16,8,256]{2,1,0:T(8,128)S(1)}, u32[]{:S(2)}, u32[]{:S(2)}) %all-to-all-start.4) | async-done | bytes 131104 | tf_op jit(solution)/shard_map/all_to_all | solution.py:308
  94.5 2.3 %update.1 = (bf16[512,1664]{1,0:T(8,128)(2,1)}, bf16[1664,256]{1,0:T(8,128)(2,1)}) custom-call(bf16[512,256]{1,0:T(8,128)(2,1)S(1)} %get-tuple-element.17.ortho_ref, bf16[1664,256]{1,0:T(8,128)(2,1)S(1)} %get-tuple-element.14.proj_ref, f32[256,256]{1,0:T(8,128)S(1)} %get-tuple-element.15.inv_ref, f32[16,8,256]{2,1,0:T(8,128)S(1)} %all-to-all-done.4.colsq_ref), custom_call_target="tpu_custom_call" | custom-call | bytes 1048576 | tf_op jit(solution)/shard_map/update/pallas_call | solution.py:42
  (1 shorter events, 0.0 us)
Async XLA Ops:
  76.9 17.5 %all-to-all-start.4 = ((f32[16,8,256]{2,1,0:T(8,128)}), f32[16,8,256]{2,1,0:T(8,128)S(1)}, u32[]{:S(2)}, u32[]{:S(2)}) async-start(f32[16,8,256]{2,1,0:T(8,128)} %get-tuple-element.18), calls=%async_computation.4 | async-start | bytes 262144 | tf_op jit(solution)/shard_map/all_to_all | solution.py:308

commit v2 on v1

--- a/solution.py
+++ b/solution.py
@@ -17,7 +17,10 @@
 HBM = pl.BlockSpec(memory_space=pltpu.HBM)
 TERMS = 2
 ORDERS = {
-    "fsdp": [2, 11, 3, 10, 0, 4, 15, 7, 12, 1, 13, 5, 14, 9, 6, 8],
+    "fsdp": [
+        [2, 11, 3, 10, 0, 4, 15, 7, 12, 1, 13, 5, 14, 9, 6, 8],
+        [2, 8, 13, 12, 1, 9, 6, 5, 11, 4, 15, 3, 10, 7, 0, 14],
+    ],
     "tp": [11, 15, 9, 1, 12, 2, 14, 10, 0, 4, 7, 6, 13, 5, 3, 8],
 }
 ROWS_BY_ROWS = (((0,), (0,)), ((), ()))
@@ -305,7 +308,10 @@
     some, block = rank // n_fsdp, cols // n_fsdp
 
     def exchange(parts, axis):
-        return lax.all_to_all(parts, axis, 0, 0, tiled=True, axis_index_groups=[ORDERS[axis]])
+        if axis == "tp":
+            return lax.all_to_all(parts, axis, 0, 0, tiled=True, axis_index_groups=[ORDERS[axis]])
+        groups = [[n_tp * f + t for f in ORDERS[axis][t % 2]] for t in range(n_tp)]
+        return lax.all_to_all(parts, ("fsdp", "tp"), 0, 0, tiled=True, axis_index_groups=groups)
 
     blended, left = blend(momentum, gradient, basis)
     parts = exchange(left.reshape(n_tp, rows // n_tp, rank), "tp")

time: 97.3 us -> 97.3 us (level)
    all_to_all x4 -> x2, blocking collectives: 69.1 us -> 30.9 us  [exchange(): lax.all_to_all(parts, axis, 0, 0, tiled=True, axis_index_groups=[ORDERS[a...]
    all_to_all x0 -> x2, blocking collectives: none -> 38.2 us  [exchange(): lax.all_to_all(parts, ('fsdp', 'tp'), 0, 0, tiled=True, axis_index_groups...]
where the time goes in v2:
time: 97.3 us; the launch traced here: 96.9 us
  blocking collectives  69.1 us (71%)
  starting transfers between devices  13.1 us (13%)
  Pallas kernels  12.2 us (13%)
  waiting for transfers between devices  1.69 us (2%)
    all_to_all x2, blocking collectives, exchange(): lax.all_to_all(parts, ('fsdp', 'tp'), 0, 0, tiled=True, axis_index_groups...  38.2 us
    all_to_all x2, blocking collectives, exchange(): lax.all_to_all(parts, axis, 0, 0, tiled=True, axis_index_groups=[ORDERS[a...  30.9 us
    all_to_all x1, starting transfers between devices, exchange(): lax.all_to_all(parts, axis, 0, 0, tiled=True, axis_index_groups=[ORDERS[a...  13.1 us
    pallas_call x6, Pallas kernels, call(): pl.pallas_call(body, out_shape=out, in_specs=[VMEM] * len(args), out_spec...  9.37 us
    pallas_call x1, Pallas kernels, blend(): pl.pallas_call(blend_body, out_shape=[held((rows, cols), BF16), held((row...  2.84 us
  transfers between devices with their start and end apart: 1, of which 1 were waited for; matrix products, arithmetic and copies ran while one was open for 0% of the time, Pallas kernels for 3%

profile of v2, /device:TPU:1, one launch (start us, length us, event | category | flops | bytes accessed | tf_op | source)
XLA Modules:
  0.0 96.9 jit_solution(3908896603500554944)
XLA Ops:
  0.6 2.8 %blend.1 = (bf16[512,1664]{1,0:T(8,128)(2,1)S(1)}, bf16[512,256]{1,0:T(8,128)(2,1)S(1)}) custom-call(bf16[512,1664]{1,0:T(8,128)(2,1)} %momentum_ref.1, bf16[512,1664]{1,0:T(8,128)(2,1)} %gradient_ref.1, bf16[1664,256]{1,0:T(8,128)(2,1)} %basis_ref.1), custom_call_target="tpu_custom_call" | custom-call | tf_op jit(solution)/shard_map/blend/pallas_call | solution.py:106
  3.5 16.9 %all_to_all.25.parts_ref = bf16[16,32,256]{2,1,0:T(8,128)(2,1)S(1)} all-to-all(bf16[16,32,256]{2,1,0:T(8,128)(2,1)S(1)} %bitcast.4), channel_id=1, replica_groups={{11,15,9,1,12,2,14,10,0,4,7,6,13,5,3,8},{27,31,25,17,28,18,30,26,16,20,..., dimensions={0} | all-to-all | bytes 524288 | tf_op jit(solution)/shard_map/all_to_all | solution.py:312
  20.4 14.0 %all_to_all.26 = bf16[16,32,256]{2,1,0:T(8,128)(2,1)S(1)} all-to-all(bf16[16,32,256]{2,1,0:T(8,128)(2,1)S(1)} %left_sum.1), channel_id=1, replica_groups={{11,15,9,1,12,2,14,10,0,4,7,6,13,5,3,8},{27,31,25,17,28,18,30,26,16,20,..., dimensions={0} | all-to-all | bytes 524288 | tf_op jit(solution)/shard_map/all_to_all | solution.py:312
  34.4 0.7 project.1
  35.1 21.0 %all_to_all.27.parts_ref = bf16[16,136,256]{2,1,0:T(8,128)(2,1)S(1)} all-to-all(bf16[16,136,256]{2,1,0:T(8,128)(2,1)S(1)} %project.1), channel_id=1, replica_groups={{32,176,48,160,0,64,240,112,192,16,208,80,224,144,96,128},{33,129,209,1..., dimensions={0} | all-to-all | bytes 2228224 | tf_op jit(solution)/shard_map/all_to_all | solution.py:314
  56.1 0.2 project_sum.1
  56.3 17.2 %all_to_all.28.parts_ref = bf16[16,136,256]{2,1,0:T(8,128)(2,1)S(1)} all-to-all(bf16[16,136,256]{2,1,0:T(8,128)(2,1)S(1)} %project_sum.1), channel_id=1, replica_groups={{32,176,48,160,0,64,240,112,192,16,208,80,224,144,96,128},{33,129,209,1..., dimensions={0} | all-to-all | bytes 2228224 | tf_op jit(solution)/shard_map/all_to_all | solution.py:314
  73.5 3.4 %factor.1 = (f32[256,256]{1,0:T(8,128)S(1)}, bf16[1664,256]{1,0:T(8,128)(2,1)S(1)}, f32[16,8,256]{2,1,0:T(8,128)}) custom-call(bf16[16,136,256]{2,1,0:T(8,128)(2,1)S(1)} %all_to_all.28.parts_ref), custom_call_target="tpu_custom_call" | custom-call | bytes 1048576 | tf_op jit(solution)/shard_map/factor/pallas_call | solution.py:45
  76.9 13.1 %all-to-all-start.4 = ((f32[16,8,256]{2,1,0:T(8,128)}), f32[16,8,256]{2,1,0:T(8,128)S(1)}, u32[]{:S(2)}, u32[]{:S(2)}) async-start(f32[16,8,256]{2,1,0:T(8,128)} %get-tuple-element.18), calls=%async_computation.4 | async-start | bytes 262144 | tf_op jit(solution)/shard_map/all_to_all | solution.py:312
  90.0 2.8 %feedback.1 = (bf16[512,1664]{1,0:T(8,128)(2,1)}, bf16[512,256]{1,0:T(8,128)(2,1)S(1)}) custom-call(bf16[512,1664]{1,0:T(8,128)(2,1)S(1)} %get-tuple-element.12.blended_ref, bf16[512,256]{1,0:T(8,128)(2,1)S(1)} %bitcast.3, bf16[1664,256]{1,0:T(8,128)(2,1)S(1)} %get-tuple-element.14.proj_ref, f32[256,256]{1,0:T(8,128)S(1)} %get-tuple-element.15.inv_ref), custom_call_target="tpu_custom_call" | custom-call | bytes 1048576 | tf_op jit(solution)/shard_map/feedback/pallas_call | solution.py:45
  92.8 1.7 %all-to-all-done.4.colsq_ref = f32[16,8,256]{2,1,0:T(8,128)S(1)} async-done(((f32[16,8,256]{2,1,0:T(8,128)}), f32[16,8,256]{2,1,0:T(8,128)S(1)}, u32[]{:S(2)}, u32[]{:S(2)}) %all-to-all-start.4) | async-done | bytes 131104 | tf_op jit(solution)/shard_map/all_to_all | solution.py:312
  94.5 2.3 %update.1 = (bf16[512,1664]{1,0:T(8,128)(2,1)}, bf16[1664,256]{1,0:T(8,128)(2,1)}) custom-call(bf16[512,256]{1,0:T(8,128)(2,1)S(1)} %get-tuple-element.17.ortho_ref, bf16[1664,256]{1,0:T(8,128)(2,1)S(1)} %get-tuple-element.14.proj_ref, f32[256,256]{1,0:T(8,128)S(1)} %get-tuple-element.15.inv_ref, f32[16,8,256]{2,1,0:T(8,128)S(1)} %all-to-all-done.4.colsq_ref), custom_call_target="tpu_custom_call" | custom-call | bytes 1048576 | tf_op jit(solution)/shard_map/update/pallas_call | solution.py:45
  (1 shorter events, 0.0 us)
Async XLA Ops:
  76.9 17.6 %all-to-all-start.4 = ((f32[16,8,256]{2,1,0:T(8,128)}), f32[16,8,256]{2,1,0:T(8,128)S(1)}, u32[]{:S(2)}, u32[]{:S(2)}) async-start(f32[16,8,256]{2,1,0:T(8,128)} %get-tuple-element.18), calls=%async_computation.4 | async-start | bytes 262144 | tf_op jit(solution)/shard_map/all_to_all | solution.py:312
